TPU v7x, 32 devices: a whole 2x2x4 slice. The times are simulated.
32 devices in a mesh: bus: 2 (over y), line: 2 (over x), scen: 8 (over z, core).
Axes of the slice: x: 2, y: 2, z: 4, core: 2. Of those that a mesh axis runs over, the one named last changes fastest.
Arguments:
- shift_factors: bfloat16 [12288, 8192], P('line', 'bus'), may hold values from -0.0625 to 0.0625
- net_load: bfloat16 [512, 8, 8192], P('scen', None, 'bus'), may hold values from -6 to 6
- dispatch_level: float32 [512, 8], P('scen'), may hold values from 0.3 to 1.5
- scenario_weight: float32 [512], P('scen'), may hold values from 0.5 to 2
- cluster_id: int32 [512, 1], P('scen'), may hold values from 0 to 63
- commitment: int32 [8, 4096], P(None, 'bus'), may hold values 0 or 1
- unit_capacity: float32 [4096], P('bus'), may hold values from 0.5 to 4
- unit_bus: int32 [4096], P('bus'), may hold values from 0 to 8191
- line_limit: float32 [12288], P('line'), may hold values from 0.3 to 1.5
- multipliers: float32 [64, 12288], P('scen', 'line'), may hold values from 0 to 1
- penalty_target: float32 [64], P('scen'), may hold values from 1 to 16
Outputs:
- new_multipliers: float32 [64, 12288], P('scen', 'line')
- cut_slopes: float32 [64, 8, 8192], P(('line', 'scen'), None, 'bus')
All inputs are finite; a program needn't handle non-finite values. No bound on the sum of `commitment` on one device may be relied on, other than what follows from the above.
Results may differ from a plain program's by a relative error of at most 0.0011.
Values may be sent and summed in bfloat16 or wider, within the bound.
A program may use at most 128 MiB of HBM per device.

v0:
```python
import jax
import jax.numpy as jnp
from jax import lax
from jax.sharding import PartitionSpec as P

BUSES = 8192
CLUSTERS = 64


step_size = 0.1


def per_device(
    shift_factors,
    net_load,
    dispatch_level,
    scenario_weight,
    cluster_id,
    commitment,
    unit_capacity,
    unit_bus,
    line_limit,
    multipliers,
    penalty_target,
):
    highest = lax.Precision.HIGHEST
    line_count, bus_count = shift_factors.shape
    scen_count, hour_count, _ = net_load.shape
    column_count = scen_count * hour_count
    values = commitment.astype(jnp.float32) * unit_capacity[None, :]
    spread = jax.ops.segment_sum(values.T, unit_bus, num_segments=BUSES).T
    capacity = lax.psum_scatter(spread, "bus", scatter_dimension=1, tiled=True)
    injection = (
        capacity[None, :, :] * dispatch_level[:, :, None] - net_load.astype(jnp.float32)
    ).astype(jnp.bfloat16)
    injection = injection.reshape(column_count, bus_count)
    member = (cluster_id == jnp.arange(CLUSTERS, dtype=jnp.int32)[None, :]).astype(jnp.float32)
    share = line_count // lax.axis_size("bus")
    block = shift_factors
    flow = lax.psum_scatter(
        lax.dot_general(
            block, injection, (((1,), (1,)), ((), ())), preferred_element_type=jnp.float32
        ),
        "bus",
        scatter_dimension=0,
        tiled=True,
    )
    first_line = lax.axis_index("bus") * share
    bounds = lax.dynamic_slice_in_dim(line_limit, first_line, share, 0)
    flow_cube = flow.reshape(flow.shape[0], scen_count, hour_count)
    edges = bounds[:, None, None]
    excess = flow_cube - jnp.clip(flow_cube, -edges, edges)
    current = lax.dynamic_slice_in_dim(multipliers, first_line, share, 1)
    penalty = 0.5 * jnp.sum(excess * excess, axis=2) * scenario_weight[None, :]
    pooled = lax.psum_scatter(
        jnp.dot(member.T, penalty.T, precision=highest), "scen", scatter_dimension=0, tiled=True
    )
    owned = jnp.maximum(current + step_size * (pooled - penalty_target[:, None]), 0.0)
    every_dual = lax.all_gather(owned, "scen", axis=0, tiled=True)
    owned, every_dual = (owned, every_dual)
    chosen = jnp.dot(member, every_dual, precision=highest)
    factor = (chosen.T * scenario_weight[None, :])[:, :, None]
    push = (excess * factor).astype(jnp.bfloat16).reshape(excess.shape[0], column_count)
    block = shift_factors
    sensitivity = lax.dot_general(
        lax.all_gather(push, "bus", axis=0, tiled=True),
        block,
        (((0,), (0,)), ((), ())),
        preferred_element_type=jnp.float32,
    )
    dual_out = lax.all_gather(owned, "bus", axis=1, tiled=True)
    scaled = (
        sensitivity.reshape(scen_count, hour_count, bus_count) * dispatch_level[:, :, None]
    ).reshape(scen_count, hour_count * bus_count)
    member_rows = member.T
    owner_count = CLUSTERS // (lax.axis_size("line") * lax.axis_size("scen"))
    slopes = lax.psum_scatter(
        jnp.dot(member_rows, scaled, precision=highest),
        ("line", "scen"),
        scatter_dimension=0,
        tiled=True,
    )
    return (dual_out, slopes.reshape(owner_count, hour_count, bus_count))


def solution(mesh):
    placed = (
        P("line", "bus"),
        P("scen", None, "bus"),
        P("scen", None),
        P("scen"),
        P("scen", None),
        P(None, "bus"),
        P("bus"),
        P("bus"),
        P("line"),
        P("scen", "line"),
        P("scen"),
    )
    return jax.shard_map(
        per_device,
        mesh=mesh,
        in_specs=placed,
        out_specs=(P("scen", "line"), P(("line", "scen"), None, "bus")),
        check_vma=False,
    )
```

profile of v0, /device:TPU:0, one launch (start us, length us, event | category | flops | bytes accessed | tf_op | source)
XLA Modules:
  0.0 637.7 jit_solution(8331931214527035547)
XLA Ops:
  7.2 0.0 copy-start.3
  7.2 0.0 reduce-scatter.4.cloned.1.call-start
  7.2 0.9 multiply_bitcast_fusion
  8.1 0.3 copy.16
  8.4 13.7 %scatter_custom_fusion = f32[8192,8]{1,0:T(8,128)} fusion(s32[2048]{0:T(1024)} %param.18, f32[2048,8]{1,0:T(8,128)S(1)} %copy.16, f32[]{:T(128)} %constant.5.clone.1), kind=kCustom, calls=%fused_computation.16 | custom fusion | flops 16384 | bytes 262656 | tf_op jit(solution)/shard_map/scatter-add | solution.py:31
  22.2 0.0 reduce-scatter.4.cloned.1.call-update
  22.2 0.0 reduce-scatter.6.cloned.1.call-start
  22.2 0.0 copy-done.3
  22.2 0.1 copy.18
  22.3 57.0 %reduce-scatter.4.cloned.1.call-done = f32[8,4096]{0,1:T(8,128)} async-done(((f32[8,8192]{0,1:T(8,128)}), f32[8,4096]{0,1:T(8,128)}) %reduce-scatter.4.cloned.1.call-update) | async-done | bytes 131088 | tf_op jit(solution)/shard_map/reduce_scatter | solution.py:32
  79.3 2.2 copy.17
  81.5 34.7 %convolution_bitcast_fusion = f32[6144,512]{0,1:T(8,128)} fusion(bf16[6144,4096]{1,0:T(8,128)(2,1)} %param.11, bf16[64,8,4096]{2,1,0:T(8,128)(2,1)} %param.12, f32[64,8]{1,0:T(8,128)S(1)} %copy.18, f32[8,4096]{1,0:T(8,128)S(1)} %copy.17), kind=kOutput, calls=%fused_computation.1 | convolution fusion | flops 25778192384 | bytes 67241984 | tf_op jit(solution)/shard_map/dot_general | solution.py:41
  116.2 0.0 reduce-scatter.6.cloned.1.call-update
  116.2 0.0 copy-start.2
  116.2 0.0 copy-start
  116.2 0.0 copy-start.4
  116.3 0.0 reduce-scatter.8.cloned.1.call-start
  116.3 0.6 copy-done.1
  116.9 0.0 copy-done.5
  116.9 143.9 %reduce-scatter.6.cloned.1.call-done = f32[3072,512]{0,1:T(8,128)} async-done(((f32[6144,512]{0,1:T(8,128)}), f32[3072,512]{0,1:T(8,128)}) %reduce-scatter.6.cloned.1.call-update) | async-done | bytes 6291472 | tf_op jit(solution)/shard_map/reduce_scatter | solution.py:40
  260.8 5.2 fusion.5
  266.1 0.0 copy-done.2
  266.1 1.5 fusion.12
  267.6 0.0 reduce-scatter.8.cloned.1.call-update
  267.6 0.0 all-gather.2.cloned.1.call-start
  267.7 31.6 %reduce-scatter.8.cloned.1.call-done = f32[8,3072]{1,0:T(8,128)} async-done(((f32[64,3072]{1,0:T(8,128)}), f32[8,3072]{1,0:T(8,128)}) %reduce-scatter.8.cloned.1.call-update) | async-done | bytes 98320 | tf_op jit(solution)/shard_map/reduce_scatter | solution.py:55
  299.3 0.0 copy-done
  299.3 0.0 copy-done.4
  299.3 1.0 add_maximum_fusion
  300.3 16.0 %all_gather.10 = f32[64,3072]{1,0:T(8,128)S(1)} all-gather(f32[8,3072]{1,0:T(8,128)S(1)} %add_maximum_fusion), channel_id=1, replica_groups=mesh['bus'=2,'line'=2,'scen'=8] {'scen'}, dimensions={0}, use_global_device_ids=true | all-gather | bytes 884736 | tf_op jit(solution)/shard_map/all_gather | solution.py:59
  316.3 0.5 convolution_multiply_fusion
  316.8 4.7 fusion.2
  321.5 0.0 all-gather.2.cloned.1.call-update
  321.5 0.0 all-reduce.3.cloned.1.call-start
  321.6 0.6 mul.79
  322.2 8.9 %copy.19 = f32[8,8,8,4096]{3,1,2,0:T(8,128)} copy(f32[8,8,8,4096]{3,2,1,0:T(8,128)S(1)} %bitcast.36) | data formatting | bytes 16777216
  331.1 69.2 %all-gather.2.cloned.1.call-done = bf16[6144,512]{0,1:T(8,128)(2,1)} async-done(((bf16[3072,512]{0,1:T(8,128)(2,1)}), bf16[6144,512]{0,1:T(8,128)(2,1)}) %all-gather.2.cloned.1.call-update) | async-done | bytes 6291472 | tf_op jit(solution)/shard_map/all_gather | solution.py:66
  400.3 34.3 %fusion.19 = f32[512,4096]{1,0:T(8,128)} fusion(bf16[6144,512]{0,1:T(8,128)(2,1)} %all-gather.2.cloned.1.call-done, bf16[6144,4096]{1,0:T(8,128)(2,1)} %param.11), kind=kOutput, calls=%fused_computation.31 | convolution fusion | flops 25769803776 | bytes 65011712 | tf_op jit(solution)/shard_map/dot_general | solution.py:65
  434.6 9.4 %reshape.32 = f32[64,32768]{1,0:T(8,128)} reshape(f32[512,4096]{1,0:T(8,128)} %fusion.19) | data formatting | bytes 16777216 | tf_op jit(solution)/shard_map/reshape | solution.py:73
  444.0 13.9 %fusion = f32[64,32768]{1,0:T(8,128)} fusion(f32[64,32768]{1,0:T(8,128)} %reshape.32, f32[64,32768]{1,0:T(8,128)} %bitcast.35, s32[64]{0:T(128)S(1)} %bitcast.42), kind=kOutput, calls=%fused_computation.2 | convolution fusion | flops 1612713984 | bytes 25166080 | tf_op jit(solution)/shard_map/dot_general | solution.py:78
  458.0 0.0 all-reduce.3.cloned.1.call-update
  458.0 0.6 copy-done.6
  458.6 0.6 dynamic-slice
  459.8 5.3 all_gather.9
  465.1 162.9 %all-reduce.3.cloned.1.call-done = f32[64,32768]{1,0:T(8,128)} async-done(((f32[64,32768]{1,0:T(8,128)}), f32[64,32768]{1,0:T(8,128)}) %all-reduce.3.cloned.1.call-update) | async-done | bytes 8388624
  628.1 1.3 constant_dynamic-slice_fusion
  629.4 1.1 copy.22
  630.5 0.7 copy.25
  (5 shorter events, 0.0 us)
Async XLA Ops:
  7.2 15.1 %copy-start.3 = (f32[64,8]{0,1:T(8,128)S(1)}, f32[64,8]{0,1:T(8,128)}, u32[]{:S(2)}) copy-start(f32[64,8]{0,1:T(8,128)} %param.13) | copy-start | bytes 6148
  7.2 72.2 %reduce-scatter.4.cloned.1.call-start = ((), (), s32[]{:S(2)}) async-start(), calls=%async_computation.3 | async-start | bytes 6291456 | tf_op jit(solution)/shard_map/reduce_scatter | solution.py:32
  22.2 238.7 %reduce-scatter.6.cloned.1.call-start = ((), (), s32[]{:S(2)}) async-start(), calls=%async_computation.4 | async-start | bytes 18874368 | tf_op jit(solution)/shard_map/reduce_scatter | solution.py:40
  116.2 0.7 copy-start.1
  116.2 0.7 copy-start.5
  116.2 149.8 %copy-start.2 = (s32[64,1]{0,1:T(1,128)S(1)}, s32[64,1]{0,1:T(1,128)}, u32[]{:S(2)}) copy-start(s32[64,1]{0,1:T(1,128)} %param.15) | copy-start | bytes 772
  116.2 183.1 %copy-start = (f32[8,6144]{1,0:T(8,128)S(1)}, f32[8,6144]{1,0:T(8,128)}, u32[]{:S(2)}) copy-start(f32[8,6144]{1,0:T(8,128)} %param.20) | copy-start | bytes 589828
  116.2 183.1 %copy-start.4 = (f32[8]{0:T(128)S(1)}, f32[8]{0:T(128)}, u32[]{:S(2)}) copy-start(f32[8]{0:T(128)} %param.21) | copy-start | bytes 100
  116.3 183.0 %reduce-scatter.8.cloned.1.call-start = ((), (), s32[]{:S(2)}) async-start(), calls=%async_computation.5 | async-start | bytes 884736 | tf_op jit(solution)/shard_map/reduce_scatter | solution.py:55
  267.6 132.7 %all-gather.2.cloned.1.call-start = ((), (), s32[]{:S(2)}) async-start(), calls=%async_computation.6 | async-start | bytes 9437184 | tf_op jit(solution)/shard_map/all_gather | solution.py:66
  321.5 306.5 %all-reduce.3.cloned.1.call-start = ((), (), s32[]{:S(2)}) async-start(), calls=%async_computation.7 | async-start | bytes 16777216
  458.0 0.7 copy-start.6
Sparse Core Ops, SparseCore 0:
  22.3 56.9 reduce-scatter.3
  116.3 144.4 reduce-scatter.5
  267.8 31.5 reduce-scatter.7
  321.7 78.6 all-gather.1
  458.1 169.9 all-reduce.2
where the time goes:
time: 638 us
  waiting for transfers between devices  465 us (73%)
  matrix products  85 us (13%)
  local copies, waits for them, and re-layouts  26.4 us (4%)
  other arithmetic  25.5 us (4%)
  blocking collectives  21.3 us (3%)
  between operations  14.5 us (2%)
    unnamed x6, waiting for transfers between devices  163 us
    reduce_scatter x1, waiting for transfers between devices, per_device(): lax.psum_scatter(lax.dot_general(block, injection, (((1,), (1,)), ((), ()...  144 us
    all_gather x1, waiting for transfers between devices, per_device(): lax.all_gather(push, 'bus', axis=0, tiled=True)  69.2 us
    reduce_scatter x1, waiting for transfers between devices, per_device(): capacity = lax.psum_scatter(spread, 'bus', scatter_dimension=1, tiled=True)  57 us
    dot_general x1, matrix products, per_device(): lax.dot_general(block, injection, (((1,), (1,)), ((), ())), preferred_ele...  34.7 us
    dot_general x1, matrix products, per_device(): lax.dot_general(lax.all_gather(push, 'bus', axis=0, tiled=True), block, (...  34.3 us
    reduce_scatter x1, waiting for transfers between devices, per_device(): lax.psum_scatter(jnp.dot(member.T, penalty.T, precision=highest), 'scen',...  31.6 us
    all_gather x1, blocking collectives, per_device(): every_dual = lax.all_gather(owned, 'scen', axis=0, tiled=True)  16 us
  transfers between devices with their start and end apart: 5, of which 5 were waited for; matrix products, arithmetic and copies ran while one was open for 2% of the time, Pallas kernels for 0%

commit v1 on v0

v1 whole, which is shorter than its diff:
```python
import jax
import jax.numpy as jnp
from jax import lax
from jax.sharding import PartitionSpec as P

step_size = 0.1
LANES = 128


def shift_by(axis, amount):
    size = lax.axis_size(axis)
    return [(i, (i + amount) % size) for i in range(size)]


def halves(x):
    high = lax.reduce_precision(x, 8, 7)
    return high.astype(jnp.bfloat16), (x - high).astype(jnp.bfloat16)


def pick(x, index, axis=0):
    return lax.dynamic_index_in_dim(x, index, axis, keepdims=False)


def scatter_sum(parts, axis, kind):
    size, me = lax.axis_size(axis), lax.axis_index(axis)
    total = pick(parts, me)
    for d in range(1, size):
        sent = pick(parts, (me + d) % size).astype(kind)
        total = total + lax.ppermute(sent, axis, shift_by(axis, d)).astype(jnp.float32)
    return total


def gather(part, axis):
    size, me = lax.axis_size(axis), lax.axis_index(axis)
    if size == 2:
        other = lax.ppermute(part, axis, shift_by(axis, 1))
        first = jnp.where(me == 0, part, other)
        second = jnp.where(me == 0, other, part)
        return jnp.stack([first, second])
    return lax.all_gather(part, axis, axis=0)


def per_device(
    shift_factors,
    net_load,
    dispatch_level,
    scenario_weight,
    cluster_id,
    commitment,
    unit_capacity,
    unit_bus,
    line_limit,
    multipliers,
    penalty_target,
):
    highest, high = lax.Precision.HIGHEST, lax.Precision.HIGH
    f32, bf16 = jnp.float32, jnp.bfloat16
    lines, buses = shift_factors.shape
    scens, hours, _ = net_load.shape
    columns = scens * hours
    nb, nl, ns = lax.axis_size("bus"), lax.axis_size("line"), lax.axis_size("scen")
    me_b, me_l, me_s = lax.axis_index("bus"), lax.axis_index("line"), lax.axis_index("scen")
    own = multipliers.shape[0]
    clusters = own * ns
    group = clusters // (nl * ns)
    chunks = max([k for k in (1, 2, 4) if lines % (k * nb * LANES) == 0] or [1])
    width = lines // chunks
    sub = width // nb

    values = commitment.astype(f32) * unit_capacity[None, :]
    tops = nb * buses // LANES
    top = unit_bus // LANES == jnp.arange(tops, dtype=jnp.int32)[:, None]
    low = (unit_bus % LANES)[:, None] == jnp.arange(LANES, dtype=jnp.int32)[None, :]
    placed = jnp.where(top[None], values[:, None, :], 0.0).reshape(hours * tops, -1)
    spread = jnp.dot(placed, low.astype(f32), precision=highest)
    spread = spread.reshape(hours, nb, buses // LANES, LANES).transpose(1, 0, 2, 3)
    capacity = scatter_sum(spread, "bus", f32).reshape(hours, buses)
    injection = (
        capacity[None] * dispatch_level[:, :, None] - net_load.astype(f32)
    ).astype(bf16).reshape(columns, buses)

    owner, hour_row, slot, place = (
        lax.broadcasted_iota(jnp.int32, (ns, hours, nl, group), i) for i in range(4)
    )
    row_cluster = ((slot * ns + owner) * group + place).reshape(-1)
    row_hour = hour_row.reshape(-1)
    scen_of = jnp.repeat(cluster_id[:, 0], hours)
    weight_of = jnp.repeat(scenario_weight, hours)
    hour_of = jnp.tile(jnp.arange(hours, dtype=jnp.int32), scens)
    same = (row_cluster[:, None] == scen_of[None, :]) & (row_hour[:, None] == hour_of[None, :])
    pool = jnp.where(same, (weight_of * dispatch_level.reshape(-1))[None, :], 0.0)
    penalty_cluster = row_cluster.reshape(ns, hours, own)[:, 0].reshape(-1)
    penalty_pool = jnp.where(
        penalty_cluster[:, None] == scen_of[None, :], 0.5 * weight_of[None, :], 0.0
    )

    limits = pick(line_limit.reshape(chunks, nb, sub), me_b, 1)
    current = pick(multipliers.reshape(own, chunks, nb, sub), me_b, 2)
    everyone = lax.all_gather(current, "scen", axis=0)
    current = pick(everyone.reshape(nl, ns, group, chunks, sub), me_s, 1).reshape(own, chunks, sub)
    targets = lax.all_gather(penalty_target, "scen", axis=0)
    targets = pick(targets.reshape(nl, ns, group), me_s, 1).reshape(own)

    pairs = ns // 2
    swap = [(i, i ^ 1) for i in range(ns)]
    me_pair, me_side = me_s // 2, me_s % 2
    duals, slopes = [], None
    received = []
    for k in range(chunks):
        part = lax.dot_general(
            injection,
            shift_factors[k * width : (k + 1) * width],
            (((1,), (1,)), ((), ())),
            preferred_element_type=f32,
        )
        part = part.reshape(columns, nb, sub).transpose(1, 0, 2)
        received.append(scatter_sum(part, "bus", bf16))
    for k in range(chunks):
        flow = received[k]
        edge = limits[k][None, :]
        excess = flow - jnp.clip(flow, -edge, edge)
        pooled = jnp.dot(pool, excess, precision=high)
        penalty = jnp.dot(penalty_pool, excess * excess, precision=high)
        both = jnp.concatenate(
            [pooled.reshape(ns, hours * own, sub), penalty.reshape(ns, own, sub)], axis=1
        ).reshape(pairs, 2, (hours + 1) * own, sub)
        both = pick(both, me_side, 1) + lax.ppermute(pick(both, 1 - me_side, 1), "scen", swap)
        total = pick(both, me_pair)
        cut = hours * own
        for d in range(1, pairs):
            sent = pick(both, (me_pair + d) % pairs)
            sent = jnp.concatenate([sent[:cut].astype(bf16), *halves(sent[cut:])], axis=0)
            perm = [(i, (i + 2 * d) % ns) for i in range(ns)]
            came = lax.ppermute(sent, "scen", perm).astype(f32)
            total = total + jnp.concatenate(
                [came[:cut], came[cut : cut + own] + came[cut + own :]], axis=0
            )
        dual = jnp.maximum(
            current[:, k] + step_size * (total[cut:] - targets[:, None]), 0.0
        )
        duals.append(dual)
        pushed = total[:cut].reshape(hours, own, sub) * dual[None]
        pushed = pushed.transpose(1, 0, 2).reshape(own * hours, sub)
        packed = gather(jnp.concatenate(halves(pushed), axis=0), "bus")
        packed = packed.transpose(1, 0, 2).reshape(2 * own * hours, width)
        step = jnp.dot(
            packed, shift_factors[k * width : (k + 1) * width], preferred_element_type=f32
        )
        slopes = step if slopes is None else slopes + step
    slopes = slopes[: own * hours] + slopes[own * hours :]
    slopes = scatter_sum(slopes.reshape(nl, group, hours, buses), "line", f32)

    dual = jnp.stack(duals, axis=1).reshape(own, chunks * sub)
    every = lax.all_gather(dual, "scen", axis=0).reshape(ns, nl, group, chunks * sub)
    every = every.transpose(1, 0, 2, 3).reshape(ns, own, chunks * sub)
    mine = gather(pick(every, me_s), "bus").reshape(nb, own, chunks, sub)
    dual_out = mine.transpose(1, 2, 0, 3).reshape(own, lines)
    return dual_out, slopes


def solution(mesh):
    placed = (
        P("line", "bus"),
        P("scen", None, "bus"),
        P("scen", None),
        P("scen"),
        P("scen", None),
        P(None, "bus"),
        P("bus"),
        P("bus"),
        P("line"),
        P("scen", "line"),
        P("scen"),
    )
    return jax.shard_map(
        per_device,
        mesh=mesh,
        in_specs=placed,
        out_specs=(P("scen", "line"), P(("line", "scen"), None, "bus")),
        check_vma=False,
    )
```

time: 638 us -> 277 us (0.43)
  waiting for transfers between devices: 465 us -> 54.4 us
  starting transfers between devices: 0.21 us -> 31.7 us
  blocking collectives: 21.3 us -> 49 us
  local copies, waits for them, and re-layouts: 26.4 us -> 42.6 us
  other arithmetic: 25.5 us -> 9.61 us
  between operations: 14.5 us -> 3.09 us
    reduce_scatter x3 -> x0, waiting for transfers between devices: 233 us -> none  [the longest x1 144 us: per_device(): lax.psum_scatter(lax.dot_general(block, injection, (((1,), (1,)), ((), ()...]
    unnamed x6 -> x0, waiting for transfers between devices: 163 us -> none
    all_gather x1 -> x0, waiting for transfers between devices: 69.2 us -> none  [per_device(): lax.all_gather(push, 'bus', axis=0, tiled=True)]
    ppermute x0 -> x27, waiting for transfers between devices: none -> 54.4 us  [the longest x6 26.9 us: scatter_sum(): lax.ppermute(sent, axis, shift_by(axis, d)).astype(jnp.float32)]
    slice x0 -> x15, local copies, waits for them, and re-layouts: none -> 33.8 us  [the longest x1 33.5 us: per_device(): shift_factors[k * width:(k + 1) * width]]
    ppermute x0 -> x27, starting transfers between devices: none -> 31.7 us  [the longest x12 19 us: per_device(): came = lax.ppermute(sent, 'scen', perm).astype(f32)]
    unnamed x0 -> x1, blocking collectives: none -> 17.5 us
    scatter-add x1 -> x0, other arithmetic: 13.7 us -> none  [per_device(): spread = jax.ops.segment_sum(values.T, unit_bus, num_segments=BUSES).T]
  transfers between devices with their start and end apart: 5 -> 27, of which waited for: 5 -> 8; matrix products, arithmetic and copies ran while one was open for 2% -> 42% of each run, Pallas kernels for 0% -> 0%
where the time goes in v1:
time: 277 us; the launch traced here: 272 us
  matrix products  82.1 us (30%)
  waiting for transfers between devices  54.4 us (20%)
  blocking collectives  49 us (18%)
  local copies, waits for them, and re-layouts  42.6 us (15%)
  starting transfers between devices  31.7 us (11%)
  other arithmetic  9.61 us (3%)
  between operations  3.09 us (1%)
    dot_general x4, matrix products, per_device(): lax.dot_general(injection, shift_factors[k * width:(k + 1) * width], (((1...  41.3 us
    slice x1, local copies, waits for them, and re-layouts, per_device(): shift_factors[k * width:(k + 1) * width]  33.5 us
    ppermute x6, waiting for transfers between devices, scatter_sum(): lax.ppermute(sent, axis, shift_by(axis, d)).astype(jnp.float32)  26.9 us
    ppermute x12, waiting for transfers between devices, per_device(): came = lax.ppermute(sent, 'scen', perm).astype(f32)  25.6 us
    dot_general x4, matrix products, per_device(): jnp.dot(packed, shift_factors[k * width:(k + 1) * width], preferred_eleme...  22.6 us
    ppermute x12, starting transfers between devices, per_device(): came = lax.ppermute(sent, 'scen', perm).astype(f32)  19 us
    unnamed x1, blocking collectives  17.5 us
    all_gather x1, blocking collectives, per_device(): everyone = lax.all_gather(current, 'scen', axis=0)  15.8 us
  transfers between devices with their start and end apart: 27, of which 8 were waited for; matrix products, arithmetic and copies ran while one was open for 42% of the time, Pallas kernels for 0%

profile of v1, /device:TPU:0, one launch (start us, length us, event | category | flops | bytes accessed | tf_op | source)
XLA Modules:
  0.0 272.4 jit_solution(3139063469541433148)
XLA Ops:
  1.5 0.9 convert_multiply_fusion
  2.4 2.4 fusion.1
  4.8 3.0 %collective-permute-start = (f32[8,32,128]{2,1,0:T(8,128)S(1)}, f32[8,32,128]{2,1,0:T(8,128)S(1)}, u32[]{:S(2)}, u32[]{:S(2)}) collective-permute-start(f32[8,32,128]{2,1,0:T(8,128)S(1)} %dynamic-slice_bitcast_fusion.1), channel_id=1, source_target_pairs={{0,16},{16,0},{1,17},{17,1},{2,18},{18,2},{3,19},{19,3},{4,20},{20... | collective-permute-start | bytes 393224 | tf_op jit(solution)/shard_map/ppermute | solution.py:29
  8.1 33.5 %fusion.177 = (bf16[1536,4096]{1,0:T(8,128)(2,1)}, bf16[1536,4096]{1,0:T(8,128)(2,1)}, bf16[1536,4096]{1,0:T(8,128)(2,1)}, bf16[1536,4096]{1,0:T(8,128)(2,1)}) fusion(bf16[6144,4096]{1,0:T(8,128)(2,1)} %param.11), kind=kLoop, calls=%fused_computation.349 | loop fusion | bytes 100663296 | tf_op jit(solution)/shard_map/slice | solution.py:112
  43.4 15.8 %all-gather = f32[64,4,1,768]{3,1,2,0:T(4,128)S(1)} all-gather(f32[8,4,1,768]{3,1,2,0:T(4,128)S(1)} %copy.95), channel_id=2, replica_groups=mesh['bus'=2,'line'=2,'scen'=8] {'scen'}, dimensions={0}, use_global_device_ids=true | all-gather | bytes 884736 | tf_op jit(solution)/shard_map/all_gather | solution.py:99
  60.7 17.5 %all-reduce.1 = f32[2,8,4]{2,1,0:T(8,128)S(1)} all-reduce(f32[2,8,4]{2,1,0:T(8,128)S(1)} %reshape.308), channel_id=3, replica_groups=mesh['bus'=2,'line'=2,'scen'=8] {'scen'}, use_global_device_ids=true, to_apply=%add | all-reduce | flops 64 | bytes 512
  78.5 10.8 %fusion.24 = f32[512,2,768]{2,0,1:T(8,128)S(1)} fusion(bf16[2,768,4096]{2,1,0:T(8,128)(2,1)} %bitcast.331, bf16[64,8,4096]{2,1,0:T(8,128)(2,1)} %param.12, f32[64,8]{1,0:T(8,128)S(1)} %copy.98, f32[8,4096]{1,0:T(8,128)S(1)} %bitcast.365), kind=kOutput, calls=%fused_computation.58 | convolution fusion | flops 6450839552 | bytes 20056064 | tf_op jit(solution)/shard_map/dot_general | solution.py:110
  90.0 0.9 copy-done.4
  91.0 10.9 %fusion.26 = f32[512,2,768]{2,0,1:T(8,128)S(1)} fusion(bf16[2,768,4096]{2,1,0:T(8,128)(2,1)} %bitcast.330, bf16[64,8,4096]{2,1,0:T(8,128)(2,1)} %param.12, f32[64,8]{1,0:T(8,128)S(1)} %copy.98, f32[8,4096]{1,0:T(8,128)S(1)} %bitcast.366), kind=kOutput, calls=%fused_computation.59 | convolution fusion | flops 6450839552 | bytes 20056064 | tf_op jit(solution)/shard_map/dot_general | solution.py:110
  102.6 0.9 copy-done.2
  103.5 10.9 %fusion.28 = f32[512,2,768]{2,0,1:T(8,128)S(1)} fusion(bf16[2,768,4096]{2,1,0:T(8,128)(2,1)} %bitcast.329, bf16[64,8,4096]{2,1,0:T(8,128)(2,1)} %param.12, f32[64,8]{1,0:T(8,128)S(1)} %copy.98, f32[8,4096]{1,0:T(8,128)S(1)} %bitcast.367), kind=kOutput, calls=%fused_computation.60 | convolution fusion | flops 6450839552 | bytes 20056064 | tf_op jit(solution)/shard_map/dot_general | solution.py:110
  115.1 0.9 copy-done
  116.1 8.8 %fusion.30 = f32[512,2,768]{2,0,1:T(8,128)S(1)} fusion(bf16[2,768,4096]{2,1,0:T(8,128)(2,1)S(1)} %bitcast.328, bf16[64,8,4096]{2,1,0:T(8,128)(2,1)} %param.12, f32[64,8]{1,0:T(8,128)S(1)} %copy.98, f32[8,4096]{1,0:T(8,128)S(1)} %bitcast.368), kind=kOutput, calls=%fused_computation.61 | convolution fusion | flops 6450839552 | bytes 20056064 | tf_op jit(solution)/shard_map/dot_general | solution.py:110
  125.6 2.7 fusion.14
  128.3 3.0 %fusion.6 = f32[512,768]{1,0:T(8,128)S(1)} fusion(bf16[512,768]{1,0:T(8,128)(2,1)} %collective-permute-done.16, f32[512,2,768]{2,0,1:T(8,128)S(1)} %copy-done.5, s32[]{:T(128)S(6)} %select_n.204, f32[768]{0:T(1024)S(1)} %neg.35, f32[768]{0:T(1024)S(1)} %get-tuple-element.5, f32[512]{0:T(512)S(1)} %mul.134, s32[512]{0:T(512)S(1)} %eq.128, s32[512]{0:T(512)S(1)} %eq.123, ...), kind=kOutput, calls=%fused_computation.18 | convolution fusion | flops 1210974208 | bytes 3950596 | tf_op jit(solution)/shard_map/dot_general | solution.py:122
  131.5 2.0 fusion.16
  133.5 3.0 %fusion.8 = f32[512,768]{1,0:T(8,128)S(1)} fusion(bf16[512,768]{1,0:T(8,128)(2,1)} %collective-permute-done.11, f32[512,2,768]{2,0,1:T(8,128)S(1)} %copy-done.3, s32[]{:T(128)S(6)} %select_n.204, f32[768]{0:T(1024)S(1)} %neg.34, f32[768]{0:T(1024)S(1)} %get-tuple-element.3, f32[512]{0:T(512)S(1)} %mul.134, s32[512]{0:T(512)S(1)} %eq.128, s32[512]{0:T(512)S(1)} %eq.123, ...), kind=kOutput, calls=%fused_computation.20 | convolution fusion | flops 1210974208 | bytes 3950596 | tf_op jit(solution)/shard_map/dot_general | solution.py:122
  137.1 6.3 %collective-permute-done.6 = bf16[512,768]{1,0:T(8,128)(2,1)S(1)} collective-permute-done((bf16[512,768]{1,0:T(8,128)(2,1)S(1)}, bf16[512,768]{1,0:T(8,128)(2,1)S(1)}, u32[]{:S(2)}, u32[]{:S(2)}) %collective-permute-start.6) | collective-permute-done | bytes 786464 | tf_op jit(solution)/shard_map/ppermute | solution.py:29
  143.4 1.7 fusion.10
  145.1 0.9 fusion.18
  146.1 9.8 %collective-permute-done.1 = bf16[512,768]{1,0:T(8,128)(2,1)S(1)} collective-permute-done((bf16[512,768]{1,0:T(8,128)(2,1)S(1)}, bf16[512,768]{1,0:T(8,128)(2,1)S(1)}, u32[]{:S(2)}, u32[]{:S(2)}) %collective-permute-start.1) | collective-permute-done | bytes 786464 | tf_op jit(solution)/shard_map/ppermute | solution.py:29
  156.0 0.9 fusion.20
  156.8 1.7 fusion.12
  159.3 1.9 collective-permute-done.2
  161.4 2.0 collective-permute-start.20
  164.1 3.3 %collective-permute-start.15 = (bf16[80,768]{1,0:T(8,128)(2,1)S(1)}, bf16[80,768]{1,0:T(8,128)(2,1)S(1)}, u32[]{:S(2)}, u32[]{:S(2)}) collective-permute-start(bf16[80,768]{1,0:T(8,128)(2,1)S(1)} %pad_maximum_fusion.13), channel_id=1, source_target_pairs={{0,6},{1,7},{2,0},{3,1},{4,2},{5,3},{6,4},{7,5},{8,14},{9,15},{10,... | collective-permute-start | bytes 368648 | tf_op jit(solution)/shard_map/ppermute | solution.py:134
  167.4 1.2 collective-permute-start.14
  169.1 6.4 %collective-permute-done.19 = bf16[80,768]{1,0:T(8,128)(2,1)S(1)} collective-permute-done((bf16[80,768]{1,0:T(8,128)(2,1)S(1)}, bf16[80,768]{1,0:T(8,128)(2,1)S(1)}, u32[]{:S(2)}, u32[]{:S(2)}) %collective-permute-start.19) | collective-permute-done | bytes 122912 | tf_op jit(solution)/shard_map/ppermute | solution.py:134
  176.0 6.9 %collective-permute-start.9 = (bf16[80,768]{1,0:T(8,128)(2,1)S(1)}, bf16[80,768]{1,0:T(8,128)(2,1)S(1)}, u32[]{:S(2)}, u32[]{:S(2)}) collective-permute-start(bf16[80,768]{1,0:T(8,128)(2,1)S(1)} %pad_maximum_fusion.9), channel_id=1, source_target_pairs={{0,4},{1,5},{2,6},{3,7},{4,0},{5,1},{6,2},{7,3},{8,12},{9,13},{10,... | collective-permute-start | bytes 368648 | tf_op jit(solution)/shard_map/ppermute | solution.py:134
  183.0 0.9 collective-permute-start.8
  183.9 7.1 %collective-permute-done.14 = bf16[80,768]{1,0:T(8,128)(2,1)S(1)} collective-permute-done((bf16[80,768]{1,0:T(8,128)(2,1)S(1)}, bf16[80,768]{1,0:T(8,128)(2,1)S(1)}, u32[]{:S(2)}, u32[]{:S(2)}) %collective-permute-start.14) | collective-permute-done | bytes 122912 | tf_op jit(solution)/shard_map/ppermute | solution.py:134
  191.6 1.7 collective-permute-start.4
  194.2 7.3 %collective-permute-done.9 = bf16[80,768]{1,0:T(8,128)(2,1)S(1)} collective-permute-done((bf16[80,768]{1,0:T(8,128)(2,1)S(1)}, bf16[80,768]{1,0:T(8,128)(2,1)S(1)}, u32[]{:S(2)}, u32[]{:S(2)}) %collective-permute-start.9) | collective-permute-done | bytes 122912 | tf_op jit(solution)/shard_map/ppermute | solution.py:134
  201.7 4.8 %collective-permute-done.4 = bf16[80,768]{1,0:T(8,128)(2,1)S(1)} collective-permute-done((bf16[80,768]{1,0:T(8,128)(2,1)S(1)}, bf16[80,768]{1,0:T(8,128)(2,1)S(1)}, u32[]{:S(2)}, u32[]{:S(2)}) %collective-permute-start.4) | collective-permute-done | bytes 122912 | tf_op jit(solution)/shard_map/ppermute | solution.py:134
  208.0 1.6 collective-permute-start.24
  210.4 1.6 collective-permute-start.22
  212.0 15.7 %all_gather.19 = f32[8,8,3072]{2,1,0:T(8,128)S(1)} all-gather(f32[1,8,3072]{2,1,0:T(8,128)S(1)} %bitcast.357), channel_id=1, replica_groups=mesh['bus'=2,'line'=2,'scen'=8] {'scen'}, dimensions={0}, use_global_device_ids=true | all-gather | bytes 884736 | tf_op jit(solution)/shard_map/all_gather | solution.py:154
  230.1 1.0 select_bitcast_fusion.1
  231.4 1.0 select_bitcast_fusion.3
  232.4 1.0 select_bitcast_fusion.5
  234.3 5.6 %fusion.175 = f32[128,4096]{1,0:T(8,128)S(1)} fusion(bf16[128,1536]{0,1:T(8,128)(2,1)S(1)} %bitcast.355, bf16[6144,4096]{1,0:T(8,128)(2,1)} %param.11), kind=kOutput, calls=%fused_computation.347 | convolution fusion | flops 1610612736 | bytes 15073280 | tf_op jit(solution)/shard_map/dot_general | solution.py:146
  240.0 5.7 %convolution_add_fusion.2 = f32[128,4096]{1,0:T(8,128)S(1)} fusion(f32[128,4096]{1,0:T(8,128)S(1)} %fusion.175, bf16[128,1536]{0,1:T(8,128)(2,1)S(1)} %bitcast.344, bf16[6144,4096]{1,0:T(8,128)(2,1)} %param.11), kind=kOutput, calls=%fused_computation.3 | convolution fusion | flops 1611137024 | bytes 17170432 | tf_op jit(solution)/shard_map/dot_general | solution.py:146
  245.7 5.7 %convolution_add_fusion.1 = f32[128,4096]{1,0:T(8,128)S(1)} fusion(f32[128,4096]{1,0:T(8,128)S(1)} %convolution_add_fusion.2, bf16[128,1536]{0,1:T(8,128)(2,1)S(1)} %bitcast.343, bf16[6144,4096]{1,0:T(8,128)(2,1)} %param.11), kind=kOutput, calls=%fused_computation.2 | convolution fusion | flops 1611137024 | bytes 17170432 | tf_op jit(solution)/shard_map/dot_general | solution.py:146
  251.3 5.7 %convolution_add_fusion = f32[128,4096]{1,0:T(8,128)S(1)} fusion(f32[128,4096]{1,0:T(8,128)S(1)} %convolution_add_fusion.1, bf16[128,1536]{0,1:T(8,128)(2,1)S(1)} %bitcast.342, bf16[6144,4096]{1,0:T(8,128)(2,1)} %param.11), kind=kOutput, calls=%fused_computation.1 | convolution fusion | flops 1611137024 | bytes 17170432 | tf_op jit(solution)/shard_map/dot_general | solution.py:146
  257.2 1.6 collective-permute-start.26
  258.7 0.9 broadcast_select_fusion.1
  260.3 10.8 %collective-permute-done.26 = f32[4,8,4096]{2,1,0:T(8,128)S(1)} collective-permute-done((f32[4,8,4096]{2,1,0:T(8,128)S(1)}, f32[4,8,4096]{2,1,0:T(8,128)S(1)}, u32[]{:S(2)}, u32[]{:S(2)}) %collective-permute-start.26) | collective-permute-done | bytes 524320 | tf_op jit(solution)/shard_map/ppermute | solution.py:29
  271.1 0.9 bitcast_add_fusion.4
  (211 shorter events, 18.5 us)
Async XLA Ops:
  0.6 7.2 %copy-start.8 = (f32[64,8]{0,1:T(8,128)S(1)}, f32[64,8]{0,1:T(8,128)}, u32[]{:S(2)}) copy-start(f32[64,8]{0,1:T(8,128)} %param.13) | copy-start | bytes 6148
  0.6 7.3 %copy-start.10 = (f32[64]{0:T(128)S(1)}, f32[64]{0:T(128)}, u32[]{:S(2)}) copy-start(f32[64]{0:T(128)} %param.14) | copy-start | bytes 772
  4.8 73.6 %collective-permute-start = (f32[8,32,128]{2,1,0:T(8,128)S(1)}, f32[8,32,128]{2,1,0:T(8,128)S(1)}, u32[]{:S(2)}, u32[]{:S(2)}) collective-permute-start(f32[8,32,128]{2,1,0:T(8,128)S(1)} %dynamic-slice_bitcast_fusion.1), channel_id=1, source_target_pairs={{0,16},{16,0},{1,17},{17,1},{2,18},{18,2},{3,19},{19,3},{4,20},{20... | collective-permute-start | bytes 393224 | tf_op jit(solution)/shard_map/ppermute | solution.py:29
  8.0 33.5 %copy-start.7 = (f32[6144]{0:T(1024)S(1)}, f32[6144]{0:T(1024)}, u32[]{:S(2)}) copy-start(f32[6144]{0:T(1024)} %param.19) | copy-start | bytes 73732
  8.1 33.6 %copy-start.9 = (s32[64,1]{0,1:T(1,128)S(1)}, s32[64,1]{0,1:T(1,128)}, u32[]{:S(2)}) copy-start(s32[64,1]{0,1:T(1,128)} %param.15) | copy-start | bytes 772
  8.1 35.0 %copy-start.6 = (f32[8,6144]{1,0:T(8,128)S(1)}, f32[8,6144]{1,0:T(8,128)}, u32[]{:S(2)}) copy-start(f32[8,6144]{1,0:T(8,128)} %param.20) | copy-start | bytes 589828
  41.5 17.6 %copy-start.12 = (u32[32]{0:T(128)S(1)}, u32[32]{0:T(128)}, u32[]{:S(2)}) copy-start(u32[32]{0:T(128)} %constant.234) | copy-start | bytes 388
  41.6 18.8 %copy-start.11 = (f32[8]{0:T(128)S(1)}, f32[8]{0:T(128)}, u32[]{:S(2)}) copy-start(f32[8]{0:T(128)} %param.21) | copy-start | bytes 100
  89.3 1.6 copy-start.4
  89.4 36.2 %collective-permute-start.16 = (bf16[512,768]{1,0:T(8,128)(2,1)S(1)}, bf16[512,768]{1,0:T(8,128)(2,1)}, u32[]{:S(2)}, u32[]{:S(2)}) collective-permute-start(bf16[512,768]{1,0:T(8,128)(2,1)S(1)} %fusion.55), channel_id=1, source_target_pairs={{0,16},{16,0},{1,17},{17,1},{2,18},{18,2},{3,19},{19,3},{4,20},{20... | collective-permute-start | bytes 2359304 | tf_op jit(solution)/shard_map/ppermute | solution.py:29
  91.0 25.1 %slice-start = ((s8[12582912]{0:T(1024)(128)(4,1)}), s8[4194304]{0:T(1024)(128)(4,1)S(1)}, s32[]{:S(2)}) async-start(s8[12582912]{0:T(1024)(128)(4,1)} %bitcast.326), calls=%async_computation | async-start | bytes 8388608
  91.0 25.1 %slice-start.1 = ((s8[12582912]{0:T(1024)(128)(4,1)}), s8[4194304]{0:T(1024)(128)(4,1)S(1)}, s32[]{:S(2)}) async-start(s8[12582912]{0:T(1024)(128)(4,1)} %bitcast.326), calls=%async_computation.1 | async-start | bytes 8388608
  101.9 1.6 copy-start.2
  102.0 29.5 %collective-permute-start.11 = (bf16[512,768]{1,0:T(8,128)(2,1)S(1)}, bf16[512,768]{1,0:T(8,128)(2,1)}, u32[]{:S(2)}, u32[]{:S(2)}) collective-permute-start(bf16[512,768]{1,0:T(8,128)(2,1)S(1)} %fusion.54), channel_id=1, source_target_pairs={{0,16},{16,0},{1,17},{17,1},{2,18},{18,2},{3,19},{19,3},{4,20},{20... | collective-permute-start | bytes 2359304 | tf_op jit(solution)/shard_map/ppermute | solution.py:29
  103.5 12.6 %slice-start.2 = ((s8[12582912]{0:T(1024)(128)(4,1)}), s8[4194304]{0:T(1024)(128)(4,1)S(1)}, s32[]{:S(2)}) async-start(s8[12582912]{0:T(1024)(128)(4,1)} %bitcast.326), calls=%async_computation.2 | async-start | bytes 8388608
  114.4 1.7 copy-start
  114.5 28.9 %collective-permute-start.6 = (bf16[512,768]{1,0:T(8,128)(2,1)S(1)}, bf16[512,768]{1,0:T(8,128)(2,1)S(1)}, u32[]{:S(2)}, u32[]{:S(2)}) collective-permute-start(bf16[512,768]{1,0:T(8,128)(2,1)S(1)} %fusion.53), channel_id=1, source_target_pairs={{0,16},{16,0},{1,17},{17,1},{2,18},{18,2},{3,19},{19,3},{4,20},{20... | collective-permute-start | bytes 2359304 | tf_op jit(solution)/shard_map/ppermute | solution.py:29
  124.9 3.4 %copy-start.5 = (f32[512,2,768]{2,0,1:T(8,128)S(1)}, f32[512,2,768]{2,0,1:T(8,128)}, u32[]{:S(2)}) copy-start(f32[512,2,768]{2,0,1:T(8,128)} %copy-done.4) | copy-start | bytes 9437188
  125.0 31.0 %collective-permute-start.1 = (bf16[512,768]{1,0:T(8,128)(2,1)S(1)}, bf16[512,768]{1,0:T(8,128)(2,1)S(1)}, u32[]{:S(2)}, u32[]{:S(2)}) collective-permute-start(bf16[512,768]{1,0:T(8,128)(2,1)S(1)} %fusion.52), channel_id=1, source_target_pairs={{0,16},{16,0},{1,17},{17,1},{2,18},{18,2},{3,19},{19,3},{4,20},{20... | collective-permute-start | bytes 2359304 | tf_op jit(solution)/shard_map/ppermute | solution.py:29
  128.3 3.2 %copy-start.3 = (f32[512,2,768]{2,0,1:T(8,128)S(1)}, f32[512,2,768]{2,0,1:T(8,128)}, u32[]{:S(2)}) copy-start(f32[512,2,768]{2,0,1:T(8,128)} %copy-done.2) | copy-start | bytes 9437188
  131.4 27.3 %collective-permute-start.17 = (f32[4,72,768]{2,1,0:T(8,128)S(1)}, f32[4,72,768]{2,1,0:T(8,128)S(1)}, u32[]{:S(2)}, u32[]{:S(2)}) collective-permute-start(f32[4,72,768]{2,1,0:T(8,128)S(1)} %fusion.33), channel_id=1, source_target_pairs={{0,1},{1,0},{2,3},{3,2},{4,5},{5,4},{6,7},{7,6},{8,9},{9,8},{10,11... | collective-permute-start | bytes 2654216 | tf_op jit(solution)/shard_map/ppermute | solution.py:127
  133.5 9.9 %copy-start.1 = (f32[512,2,768]{2,0,1:T(8,128)S(1)}, f32[512,2,768]{2,0,1:T(8,128)}, u32[]{:S(2)}) copy-start(f32[512,2,768]{2,0,1:T(8,128)} %copy-done) | copy-start | bytes 9437188
  136.6 22.3 %collective-permute-start.12 = (f32[4,72,768]{2,1,0:T(8,128)S(1)}, f32[4,72,768]{2,1,0:T(8,128)S(1)}, u32[]{:S(2)}, u32[]{:S(2)}) collective-permute-start(f32[4,72,768]{2,1,0:T(8,128)S(1)} %fusion.38), channel_id=1, source_target_pairs={{0,1},{1,0},{2,3},{3,2},{4,5},{5,4},{6,7},{7,6},{8,9},{9,8},{10,11... | collective-permute-start | bytes 2654216 | tf_op jit(solution)/shard_map/ppermute | solution.py:127
  146.0 13.0 %collective-permute-start.7 = (f32[4,72,768]{2,1,0:T(8,128)S(1)}, f32[4,72,768]{2,1,0:T(8,128)S(1)}, u32[]{:S(2)}, u32[]{:S(2)}) collective-permute-start(f32[4,72,768]{2,1,0:T(8,128)S(1)} %fusion.43), channel_id=1, source_target_pairs={{0,1},{1,0},{2,3},{3,2},{4,5},{5,4},{6,7},{7,6},{8,9},{9,8},{10,11... | collective-permute-start | bytes 2654216 | tf_op jit(solution)/shard_map/ppermute | solution.py:127
  158.6 2.5 collective-permute-start.2
  161.4 7.3 %collective-permute-start.20 = (bf16[80,768]{1,0:T(8,128)(2,1)S(1)}, bf16[80,768]{1,0:T(8,128)(2,1)S(1)}, u32[]{:S(2)}, u32[]{:S(2)}) collective-permute-start(bf16[80,768]{1,0:T(8,128)(2,1)S(1)} %pad_maximum_fusion.16), channel_id=1, source_target_pairs={{0,6},{1,7},{2,0},{3,1},{4,2},{5,3},{6,4},{7,5},{8,14},{9,15},{10,... | collective-permute-start | bytes 368648 | tf_op jit(solution)/shard_map/ppermute | solution.py:134
  163.3 12.2 %collective-permute-start.19 = (bf16[80,768]{1,0:T(8,128)(2,1)S(1)}, bf16[80,768]{1,0:T(8,128)(2,1)S(1)}, u32[]{:S(2)}, u32[]{:S(2)}) collective-permute-start(bf16[80,768]{1,0:T(8,128)(2,1)S(1)} %pad_maximum_fusion.15), channel_id=1, source_target_pairs={{0,4},{1,5},{2,6},{3,7},{4,0},{5,1},{6,2},{7,3},{8,12},{9,13},{10,... | collective-permute-start | bytes 368648 | tf_op jit(solution)/shard_map/ppermute | solution.py:134
  163.4 12.6 %collective-permute-start.18 = (bf16[80,768]{1,0:T(8,128)(2,1)S(1)}, bf16[80,768]{1,0:T(8,128)(2,1)S(1)}, u32[]{:S(2)}, u32[]{:S(2)}) collective-permute-start(bf16[80,768]{1,0:T(8,128)(2,1)S(1)} %pad_maximum_fusion.14), channel_id=1, source_target_pairs={{0,2},{1,3},{2,4},{3,5},{4,6},{5,7},{6,0},{7,1},{8,10},{9,11},{10,... | collective-permute-start | bytes 368648 | tf_op jit(solution)/shard_map/ppermute | solution.py:134
  164.1 18.9 %collective-permute-start.15 = (bf16[80,768]{1,0:T(8,128)(2,1)S(1)}, bf16[80,768]{1,0:T(8,128)(2,1)S(1)}, u32[]{:S(2)}, u32[]{:S(2)}) collective-permute-start(bf16[80,768]{1,0:T(8,128)(2,1)S(1)} %pad_maximum_fusion.13), channel_id=1, source_target_pairs={{0,6},{1,7},{2,0},{3,1},{4,2},{5,3},{6,4},{7,5},{8,14},{9,15},{10,... | collective-permute-start | bytes 368648 | tf_op jit(solution)/shard_map/ppermute | solution.py:134
  167.4 23.6 %collective-permute-start.14 = (bf16[80,768]{1,0:T(8,128)(2,1)S(1)}, bf16[80,768]{1,0:T(8,128)(2,1)S(1)}, u32[]{:S(2)}, u32[]{:S(2)}) collective-permute-start(bf16[80,768]{1,0:T(8,128)(2,1)S(1)} %pad_maximum_fusion.12), channel_id=1, source_target_pairs={{0,4},{1,5},{2,6},{3,7},{4,0},{5,1},{6,2},{7,3},{8,12},{9,13},{10,... | collective-permute-start | bytes 368648 | tf_op jit(solution)/shard_map/ppermute | solution.py:134
  168.7 22.9 %collective-permute-start.13 = (bf16[80,768]{1,0:T(8,128)(2,1)S(1)}, bf16[80,768]{1,0:T(8,128)(2,1)S(1)}, u32[]{:S(2)}, u32[]{:S(2)}) collective-permute-start(bf16[80,768]{1,0:T(8,128)(2,1)S(1)} %pad_maximum_fusion.11), channel_id=1, source_target_pairs={{0,2},{1,3},{2,4},{3,5},{4,6},{5,7},{6,0},{7,1},{8,10},{9,11},{10,... | collective-permute-start | bytes 368648 | tf_op jit(solution)/shard_map/ppermute | solution.py:134
  175.5 17.9 %collective-permute-start.10 = (bf16[80,768]{1,0:T(8,128)(2,1)S(1)}, bf16[80,768]{1,0:T(8,128)(2,1)S(1)}, u32[]{:S(2)}, u32[]{:S(2)}) collective-permute-start(bf16[80,768]{1,0:T(8,128)(2,1)S(1)} %pad_maximum_fusion.10), channel_id=1, source_target_pairs={{0,6},{1,7},{2,0},{3,1},{4,2},{5,3},{6,4},{7,5},{8,14},{9,15},{10,... | collective-permute-start | bytes 368648 | tf_op jit(solution)/shard_map/ppermute | solution.py:134
  176.0 25.5 %collective-permute-start.9 = (bf16[80,768]{1,0:T(8,128)(2,1)S(1)}, bf16[80,768]{1,0:T(8,128)(2,1)S(1)}, u32[]{:S(2)}, u32[]{:S(2)}) collective-permute-start(bf16[80,768]{1,0:T(8,128)(2,1)S(1)} %pad_maximum_fusion.9), channel_id=1, source_target_pairs={{0,4},{1,5},{2,6},{3,7},{4,0},{5,1},{6,2},{7,3},{8,12},{9,13},{10,... | collective-permute-start | bytes 368648 | tf_op jit(solution)/shard_map/ppermute | solution.py:134
  183.0 18.6 %collective-permute-start.8 = (bf16[80,768]{1,0:T(8,128)(2,1)S(1)}, bf16[80,768]{1,0:T(8,128)(2,1)S(1)}, u32[]{:S(2)}, u32[]{:S(2)}) collective-permute-start(bf16[80,768]{1,0:T(8,128)(2,1)S(1)} %pad_maximum_fusion.8), channel_id=1, source_target_pairs={{0,2},{1,3},{2,4},{3,5},{4,6},{5,7},{6,0},{7,1},{8,10},{9,11},{10,... | collective-permute-start | bytes 368648 | tf_op jit(solution)/shard_map/ppermute | solution.py:134
  191.0 10.7 %collective-permute-start.5 = (bf16[80,768]{1,0:T(8,128)(2,1)S(1)}, bf16[80,768]{1,0:T(8,128)(2,1)S(1)}, u32[]{:S(2)}, u32[]{:S(2)}) collective-permute-start(bf16[80,768]{1,0:T(8,128)(2,1)S(1)} %pad_maximum_fusion.7), channel_id=1, source_target_pairs={{0,6},{1,7},{2,0},{3,1},{4,2},{5,3},{6,4},{7,5},{8,14},{9,15},{10,... | collective-permute-start | bytes 368648 | tf_op jit(solution)/shard_map/ppermute | solution.py:134
  191.6 14.9 %collective-permute-start.4 = (bf16[80,768]{1,0:T(8,128)(2,1)S(1)}, bf16[80,768]{1,0:T(8,128)(2,1)S(1)}, u32[]{:S(2)}, u32[]{:S(2)}) collective-permute-start(bf16[80,768]{1,0:T(8,128)(2,1)S(1)} %pad_maximum_fusion.6), channel_id=1, source_target_pairs={{0,4},{1,5},{2,6},{3,7},{4,0},{5,1},{6,2},{7,3},{8,12},{9,13},{10,... | collective-permute-start | bytes 368648 | tf_op jit(solution)/shard_map/ppermute | solution.py:134
  193.4 13.2 %collective-permute-start.3 = (bf16[80,768]{1,0:T(8,128)(2,1)S(1)}, bf16[80,768]{1,0:T(8,128)(2,1)S(1)}, u32[]{:S(2)}, u32[]{:S(2)}) collective-permute-start(bf16[80,768]{1,0:T(8,128)(2,1)S(1)} %pad_maximum_fusion.5), channel_id=1, source_target_pairs={{0,2},{1,3},{2,4},{3,5},{4,6},{5,7},{6,0},{7,1},{8,10},{9,11},{10,... | collective-permute-start | bytes 368648 | tf_op jit(solution)/shard_map/ppermute | solution.py:134
  207.3 22.8 %collective-permute-start.25 = (bf16[128,768]{1,0:T(8,128)(2,1)S(1)}, bf16[128,768]{1,0:T(8,128)(2,1)}, u32[]{:S(2)}, u32[]{:S(2)}) collective-permute-start(bf16[128,768]{1,0:T(8,128)(2,1)S(1)} %pad_maximum_fusion.4), channel_id=1, source_target_pairs={{0,16},{16,0},{1,17},{17,1},{2,18},{18,2},{3,19},{19,3},{4,20},{20... | collective-permute-start | bytes 589832 | tf_op jit(solution)/shard_map/ppermute | solution.py:36
  208.0 23.4 %collective-permute-start.24 = (bf16[128,768]{1,0:T(8,128)(2,1)S(1)}, bf16[128,768]{1,0:T(8,128)(2,1)}, u32[]{:S(2)}, u32[]{:S(2)}) collective-permute-start(bf16[128,768]{1,0:T(8,128)(2,1)S(1)} %pad_maximum_fusion.3), channel_id=1, source_target_pairs={{0,16},{16,0},{1,17},{17,1},{2,18},{18,2},{3,19},{19,3},{4,20},{20... | collective-permute-start | bytes 589832 | tf_op jit(solution)/shard_map/ppermute | solution.py:36
  209.7 22.7 %collective-permute-start.23 = (bf16[128,768]{1,0:T(8,128)(2,1)S(1)}, bf16[128,768]{1,0:T(8,128)(2,1)}, u32[]{:S(2)}, u32[]{:S(2)}) collective-permute-start(bf16[128,768]{1,0:T(8,128)(2,1)S(1)} %pad_maximum_fusion.2), channel_id=1, source_target_pairs={{0,16},{16,0},{1,17},{17,1},{2,18},{18,2},{3,19},{19,3},{4,20},{20... | collective-permute-start | bytes 589832 | tf_op jit(solution)/shard_map/ppermute | solution.py:36
  210.4 23.6 %collective-permute-start.22 = (bf16[128,768]{1,0:T(8,128)(2,1)S(1)}, bf16[128,768]{1,0:T(8,128)(2,1)S(1)}, u32[]{:S(2)}, u32[]{:S(2)}) collective-permute-start(bf16[128,768]{1,0:T(8,128)(2,1)S(1)} %pad_maximum_fusion.1), channel_id=1, source_target_pairs={{0,16},{16,0},{1,17},{17,1},{2,18},{18,2},{3,19},{19,3},{4,20},{20... | collective-permute-start | bytes 589832 | tf_op jit(solution)/shard_map/ppermute | solution.py:36
  229.6 29.1 %collective-permute-start.21 = (f32[8,3072]{1,0:T(8,128)}, f32[8,3072]{1,0:T(8,128)}, u32[]{:S(2)}, u32[]{:S(2)}) collective-permute-start(f32[8,3072]{1,0:T(8,128)} %dynamic-slice_bitcast_fusion.2), channel_id=1, source_target_pairs={{0,16},{16,0},{1,17},{17,1},{2,18},{18,2},{3,19},{19,3},{4,20},{20... | collective-permute-start | bytes 294920 | tf_op jit(solution)/shard_map/ppermute | solution.py:36
  257.2 13.9 %collective-permute-start.26 = (f32[4,8,4096]{2,1,0:T(8,128)S(1)}, f32[4,8,4096]{2,1,0:T(8,128)S(1)}, u32[]{:S(2)}, u32[]{:S(2)}) collective-permute-start(f32[4,8,4096]{2,1,0:T(8,128)S(1)} %dynamic-slice_bitcast_fusion), channel_id=1, source_target_pairs={{0,8},{8,0},{1,9},{9,1},{2,10},{10,2},{3,11},{11,3},{4,12},{12,4},... | collective-permute-start | bytes 1572872 | tf_op jit(solution)/shard_map/ppermute | solution.py:29
